TPU v7x, 32 devices: a whole 2x2x4 slice. The times are simulated.
32 devices in a mesh: groups: 2 (over x), space: 16 (over z, y, core).
Axes of the slice: x: 2, y: 2, z: 4, core: 2. Of those that a mesh axis runs over, the one named last changes fastest.
Arguments:
- grid_latent: bfloat16 [8, 4096, 1024], P(None, ('groups', 'space')), parts along dimension 1, may hold values from -6 to 6
- mesh_latent: bfloat16 [8, 1024, 1024], P(None, ('groups', 'space')), parts along dimension 1, may hold values from -6 to 6
- query_weight: bfloat16 [1024, 1024], replicated, may hold values from -0.1875 to 0.1875
- kv_weight: bfloat16 [1024, 2048], replicated, may hold values from -0.1875 to 0.1875
- field_weight: bfloat16 [100, 1024], replicated, may hold values from -0.1875 to 0.1875
- target: float32 [100, 4096], P(None, ('groups', 'space')), parts along dimension 1, may hold values from -6 to 6
- area_weight: float32 [4096], P(('groups', 'space')), parts along dimension 0, may hold values from 1 to 36
- request: int32 [32, 16, 2], P(('groups', 'space')), parts along dimension 0, may hold values from 0 to 31, as said below
- edge_slot: int32 [3, 4096], P(None, ('groups', 'space')), parts along dimension 1, may hold values from 0 to 31, as said below
Outputs:
- mesh_grad: bfloat16 [8, 1024, 1024], P(None, ('groups', 'space')), parts along dimension 1
- mean_loss: float32 [2], P('groups'), parts along dimension 0
There are 2 independent parts, one for each index of `groups`. A program takes and returns all parts, laid end to end along the dimension named above; an argument that names none is the same for every part. Nothing has to cross between parts.
Inputs may be any that keep to these rules, and one draw needn't show every extreme that they name: request[d, s, 0] and request[d, s, 1] are two different local mesh-node indices of shard s. `edge_slot`: every slot named for shard d = g // 128 indexes that shard's own request row; the 3 slots of one grid point differ; one shard's edges name exactly 16 distinct slots: both slots of 4 source shards, slot 0 of 8 others, none of the rest.
All inputs are finite; a program needn't handle non-finite values.
Results may differ from a plain program's by a relative error of at most 0.0093.
Values may be sent and summed in bfloat16 or wider, within the bound.
A program may use at most 128 MiB of HBM per device.

v0:
```python
import functools
import math

import jax
import jax.numpy as jnp
from jax import lax
from jax.experimental import pallas as pl
from jax.experimental.pallas import tpu as pltpu
from jax.sharding import PartitionSpec as P

HEADS = 16
SMOOTHING = 0.04
FAIRNESS = 0.95
BF = jnp.bfloat16
F32 = jnp.float32


def dot(a, b, dims):
    return lax.dot_general(a, b, ((dims[:1], dims[1:]), ((), ())), preferred_element_type=F32)


def iota(shape, dim):
    return lax.broadcasted_iota(jnp.int32, shape, dim)


def order_matrix(rows, members, slots, cap):
    r, c = iota((rows, rows), 0), iota((rows, rows), 1)
    member, slot = r // slots, r % slots
    return (c == slot * members + member).astype(F32).astype(BF)


def decoder_kernel(
    members, fields, slots, cap,
    x_ref, lat_ref, qw_ref, kvw_ref, fw_ref, target_ref, area_ref, edge_ref,
    out_ref, total_ref,
    q_s, kv_s, p_s, att_s, pred_s, dp_s, da_s, sg_s,
):
    points = target_ref.shape[1]
    width = qw_ref.shape[0]
    rows = members * slots
    head_dim = width // HEADS
    group_heads = 256 // head_dim
    groups = HEADS // group_heads
    order = order_matrix(rows, members, slots, cap)
    latent = dot(order, lat_ref[...], (1, 0)).astype(BF)
    for c in range(0, 2 * width, 512):
        kv_s[:, c:c + 512] = dot(latent, kvw_ref[:, c:c + 512], (1, 0)).astype(BF)
    for c in range(0, width, 256):
        q_s[:, c:c + 256] = dot(x_ref[...], qw_ref[:, c:c + 256], (1, 0)).astype(BF)

    hs = group_heads * slots
    head_mask = (iota((hs, 256), 0) // slots == iota((hs, 256), 1) // head_dim).astype(F32)
    head_mask16 = head_mask.astype(BF)
    slot_ids = iota((slots, points), 0)
    named = (slot_ids == edge_ref[0:1, :]) | (slot_ids == edge_ref[1:2, :]) | (slot_ids == edge_ref[2:3, :])
    named = named.astype(F32)
    named = jnp.concatenate([named] * group_heads, axis=0) > 0.5

    def blocks(values):
        return jnp.concatenate([values] * group_heads, axis=0) * head_mask16

    scale = 1.0 / math.sqrt(head_dim)
    for e in range(members):
        rs = slice(e * slots, (e + 1) * slots)
        gs = slice(e * points, (e + 1) * points)
        for k in range(groups):
            cs = slice(k * 256, (k + 1) * 256)
            keys = blocks(kv_s[rs, cs])
            values = blocks(kv_s[rs, width + k * 256:width + (k + 1) * 256])
            score = dot(keys, q_s[gs, cs], (1, 1)) * scale
            exponent = jnp.where(named, jnp.exp(score), 0.0)
            by_head = exponent.reshape(group_heads, slots, points)
            total = jnp.sum(by_head, axis=1, keepdims=True)
            weight = (by_head / total).reshape(hs, points)
            p_s[e, k] = weight
            att_s[cs, gs] = dot(values, weight.astype(BF), (0, 0)).astype(BF)

    pred_s[...] = dot(fw_ref[...], att_s[...], (1, 0))

    area = area_ref[...]
    almost_fair = 1.0 - (1.0 - FAIRNESS) / members
    spread_factor = almost_fair / (members * (members - 1))
    total = jnp.zeros((8, points), F32)
    padded = fw_ref.shape[0]
    for f in range(0, padded, 8):
        fs = slice(f, f + 8)
        if f >= fields:
            dp_s[fs, :] = jnp.zeros((8, members * points), F32)
            continue
        goal = target_ref[fs, :]
        preds = [pred_s[fs, e * points:(e + 1) * points] for e in range(members)]
        slopes = []
        skill = jnp.zeros((8, points), F32)
        for e in range(members):
            u = preds[e] - goal
            v = u * u + SMOOTHING
            r = lax.rsqrt(v)
            skill += v * r
            slopes.append(u * r * (1.0 / members))
        spread = jnp.zeros((8, points), F32)
        pulls = [jnp.zeros((8, points), F32) for _ in range(members)]
        for a in range(members):
            for b in range(a + 1, members):
                u = preds[a] - preds[b]
                v = u * u + SMOOTHING
                r = lax.rsqrt(v)
                spread += v * r
                w = u * r
                pulls[a] = pulls[a] + w
                pulls[b] = pulls[b] - w
        pointwise = skill * (1.0 / members) - spread_factor * spread
        valid = iota((8, points), 0) + f < fields
        total += jnp.where(valid, pointwise * area, 0.0)
        for e in range(members):
            slope = (slopes[e] - spread_factor * pulls[e]) * area
            dp_s[fs, e * points:(e + 1) * points] = jnp.where(valid, slope, 0.0)
    total_ref[...] = total

    dp = dp_s[...].astype(BF)
    for k in range(groups):
        cs = slice(k * 256, (k + 1) * 256)
        da_s[cs, :] = dot(fw_ref[:, cs], dp, (0, 0)).astype(BF)

    def fold(product):
        kept = (product * head_mask).reshape(group_heads, slots, 256)
        return jnp.sum(kept, axis=0).astype(BF)

    for e in range(members):
        rs = slice(e * slots, (e + 1) * slots)
        gs = slice(e * points, (e + 1) * points)
        for k in range(groups):
            cs = slice(k * 256, (k + 1) * 256)
            vs = slice(width + k * 256, width + (k + 1) * 256)
            values = blocks(kv_s[rs, vs])
            weight = p_s[e, k]
            da = da_s[cs, gs]
            dw = dot(values, da, (1, 0))
            pull = (weight * dw).reshape(group_heads, slots, points)
            mean = jnp.sum(pull, axis=1, keepdims=True)
            ds = pull - weight.reshape(group_heads, slots, points) * mean
            ds = (ds.reshape(hs, points) * scale).astype(BF)
            sg_s[rs, cs] = fold(dot(ds, q_s[gs, cs], (1, 0)))
            sg_s[rs, vs] = fold(dot(weight.astype(BF), da, (1, 1)))

    latent_grad = dot(sg_s[...], kvw_ref[...], (1, 1)).astype(BF)
    out_ref[...] = dot(order, latent_grad, (0, 0)).astype(BF)


def decode(grid_latent, latent, query_weight, kv_weight, field_weight, target, area, edge_slot, members, slots, cap, fields):
    points, width = target.shape[1], query_weight.shape[0]
    padded = field_weight.shape[0]
    rows = members * slots
    group_heads = 256 * HEADS // width
    vmem = pl.BlockSpec(memory_space=pltpu.VMEM)
    return pl.pallas_call(
        functools.partial(decoder_kernel, members, fields, slots, cap),
        out_shape=(
            jax.ShapeDtypeStruct((rows, width), BF),
            jax.ShapeDtypeStruct((8, points), F32),
        ),
        in_specs=[vmem] * 8,
        out_specs=(vmem, vmem),
        scratch_shapes=[
            pltpu.VMEM((members * points, width), BF),
            pltpu.VMEM((rows, 2 * width), BF),
            pltpu.VMEM((members, HEADS // group_heads, group_heads * slots, points), F32),
            pltpu.VMEM((width, members * points), BF),
            pltpu.VMEM((padded, members * points), F32),
            pltpu.VMEM((padded, members * points), F32),
            pltpu.VMEM((width, members * points), BF),
            pltpu.VMEM((rows, 2 * width), BF),
        ],
        compiler_params=pltpu.CompilerParams(vmem_limit_bytes=56 * 1024 * 1024),
    )(grid_latent, latent, query_weight, kv_weight, field_weight, target, area, edge_slot)


def local(
    grid_latent, mesh_latent, query_weight, kv_weight, field_weight, target, area_weight, request, edge_slot,
):
    members, points, width = grid_latent.shape
    nodes = mesh_latent.shape[1]
    shards = lax.axis_size("space")
    cap = request.shape[2]
    slots = shards * cap
    per = cap * members
    fields = target.shape[0]
    incoming = lax.all_to_all(request.reshape(shards, cap), "space", split_axis=0, concat_axis=0, tiled=True)
    wanted = jnp.broadcast_to(incoming[:, :, None], (shards, cap, members)).reshape(shards * per, 1)
    member_of = iota((shards * per, members * nodes), 0) % members
    column = iota((shards * per, members * nodes), 1)
    select = (column == member_of * nodes + wanted).astype(BF)
    rows = mesh_latent.reshape(members * nodes, width)
    picked = jnp.dot(select, rows, preferred_element_type=F32).astype(BF)
    arrived = lax.all_to_all(
        picked.reshape(shards, per, width), "space", split_axis=0, concat_axis=0, tiled=True
    ).reshape(shards * per, width)
    field_pad = jnp.pad(field_weight, ((0, 128 - fields), (0, 0)))
    target_pad = jnp.pad(target, ((0, -fields % 8), (0, 0)))
    grads, total = decode(
        grid_latent.reshape(members * points, width), arrived, query_weight, kv_weight, field_pad,
        target_pad, area_weight.reshape(1, points), edge_slot, members, slots, cap, fields,
    )
    returned = lax.all_to_all(
        grads.reshape(shards, per, width), "space", split_axis=0, concat_axis=0, tiled=True
    ).reshape(shards * per, width)
    mesh_grad = lax.dot_general(
        select, returned, (((0,), (0,)), ((), ())), preferred_element_type=F32
    ).astype(BF).reshape(members, nodes, width)
    totals = lax.all_to_all(
        jnp.broadcast_to(jnp.sum(total), (shards, 128)), "space", split_axis=0, concat_axis=0, tiled=True
    )
    mean_loss = (jnp.sum(totals[:, 0]) / (fields * points * shards)).reshape(1)
    return (mesh_grad, mean_loss)


def solution(mesh):
    placed = (
        P(None, ("groups", "space"), None),
        P(None, ("groups", "space"), None),
        P(),
        P(),
        P(),
        P(None, ("groups", "space")),
        P(("groups", "space")),
        P(("groups", "space"), None, None),
        P(None, ("groups", "space")),
    )
    return jax.shard_map(
        local,
        mesh=mesh,
        in_specs=placed,
        out_specs=(P(None, ("groups", "space"), None), P("groups")),
        check_vma=False,
    )
```

profile of v0, /device:TPU:0, one launch (start us, length us, event | category | flops | bytes accessed | tf_op | source)
XLA Modules:
  0.0 86.0 jit_solution(8855196918839353566)
XLA Ops:
  0.6 0.0 copy-start
  0.6 0.0 copy-start.2
  0.7 0.0 copy-start.3
  0.7 1.4 %copy.19 = s32[16,1,2]{2,1,0:T(1,128)} copy(s32[16,1,2]{0,2,1:T(2,128)} %bitcast.22) | data formatting | bytes 256 | tf_op jit(solution)/shard_map/all_to_all | solution.py:187
  2.1 7.4 %all-to-all-start = ((s32[16,1,2]{2,1,0:T(1,128)}), s32[16,1,2]{2,1,0:T(1,128)S(1)}, u32[]{:S(2)}, u32[]{:S(2)}) async-start(s32[16,1,2]{2,1,0:T(1,128)} %copy.19), calls=%async_computation | async-start | bytes 16384 | tf_op jit(solution)/shard_map/all_to_all | solution.py:187
  9.5 6.3 %all-to-all-done = s32[16,1,2]{2,1,0:T(1,128)S(1)} async-done(((s32[16,1,2]{2,1,0:T(1,128)}), s32[16,1,2]{2,1,0:T(1,128)S(1)}, u32[]{:S(2)}, u32[]{:S(2)}) %all-to-all-start) | async-done | bytes 160 | tf_op jit(solution)/shard_map/all_to_all | solution.py:187
  15.8 0.1 broadcast_in_dim.12
  15.9 0.1 add.22
  16.0 0.0 copy-done
  16.0 1.2 %convolution_convert_fusion.1 = bf16[256,1024]{1,0:T(8,128)(2,1)} fusion(bf16[256,1024]{1,0:T(8,128)(2,1)S(1)} %bitcast.14, s32[256]{0:T(256)S(1)} %add.22, s32[256]{0:T(256)S(1)} %get-tuple-element.6, s32[256]{0:T(256)S(1)} %get-tuple-element.7, pred[256]{0:T(512)(128)(4,1)S(1)} %compare_and_fusion), kind=kOutput, calls=%fused_computation.1 | convolution fusion | flops 134742016 | bytes 1051904 | tf_op jit(solution)/shard_map/dot_general | solution.py:193
  17.2 3.6 %all-to-all-start.1 = ((bf16[16,16,1024]{2,1,0:T(8,128)(2,1)}), bf16[16,16,1024]{2,1,0:T(8,128)(2,1)S(1)}, u32[]{:S(2)}, u32[]{:S(2)}) async-start(bf16[16,16,1024]{2,1,0:T(8,128)(2,1)} %bitcast.4), calls=%async_computation.1 | async-start | bytes 1048576 | tf_op jit(solution)/shard_map/all_to_all | solution.py:194
  20.8 0.0 copy-done.2
  20.8 0.7 pad.8.fw_ref
  21.5 0.0 copy-done.3
  21.5 0.6 pad.9.target_ref
  22.1 13.1 %all-to-all-done.1 = bf16[16,16,1024]{2,1,0:T(8,128)(2,1)S(1)} async-done(((bf16[16,16,1024]{2,1,0:T(8,128)(2,1)}), bf16[16,16,1024]{2,1,0:T(8,128)(2,1)S(1)}, u32[]{:S(2)}, u32[]{:S(2)}) %all-to-all-start.1) | async-done | bytes 524320 | tf_op jit(solution)/shard_map/all_to_all | solution.py:194
  35.2 0.0 copy-start.1
  35.2 0.8 copy-done.1
  36.0 17.4 %shard_map.104 = (bf16[256,1024]{1,0:T(8,128)(2,1)}, f32[8,128]{1,0:T(8,128)}) custom-call(bf16[1024,1024]{1,0:T(8,128)(2,1)} %bitcast.15, bf16[256,1024]{1,0:T(8,128)(2,1)} %bitcast.16, bf16[1024,1024]{1,0:T(8,128)(2,1)} %qw_ref.1, bf16[1024,2048]{1,0:T(8,128)(2,1)} %kvw_ref.1, bf16[128,1024]{1,0:T(8,128)(2,1)} %pad.8.fw_ref, f32[104,128]{1,0:T(8,128)} %pad.9.target_ref, ...), custom_call_target="tpu_custom_call" | custom-call | tf_op jit(solution)/shard_map/pallas_call | solution.py:155
  53.4 1.3 %reduce_sum.18 = f32[]{:T(128)} reduce(f32[8,128]{1,0:T(8,128)} %get-tuple-element.5, f32[]{:T(128)} %constant.25.clone.1), dimensions={0,1}, to_apply=%region_0.1 | reduce | flops 1023 | bytes 4104 | tf_op jit(solution)/shard_map/reduce_sum | solution.py:210
  54.7 0.6 broadcast_in_dim.13
  55.4 10.2 %all_to_all.28 = f32[16,1,128]{2,1,0:T(1,128)S(1)} all-to-all(f32[16,1,128]{2,1,0:T(1,128)S(1)} %broadcast_in_dim.13), channel_id=1, replica_groups=mesh['groups'=2,'space'=16] {'space'}, dimensions={0} | all-to-all | bytes 16384 | tf_op jit(solution)/shard_map/all_to_all | solution.py:209
  65.6 3.6 %all-to-all-start.2 = ((bf16[16,16,1024]{2,1,0:T(8,128)(2,1)}), bf16[16,16,1024]{2,1,0:T(8,128)(2,1)S(1)}, u32[]{:S(2)}, u32[]{:S(2)}) async-start(bf16[16,16,1024]{2,1,0:T(8,128)(2,1)} %bitcast.18), calls=%async_computation.2 | async-start | bytes 1048576 | tf_op jit(solution)/shard_map/all_to_all | solution.py:203
  69.2 0.6 slice_reduce_fusion
  70.4 13.2 %all-to-all-done.2 = bf16[16,16,1024]{2,1,0:T(8,128)(2,1)S(1)} async-done(((bf16[16,16,1024]{2,1,0:T(8,128)(2,1)}), bf16[16,16,1024]{2,1,0:T(8,128)(2,1)S(1)}, u32[]{:S(2)}, u32[]{:S(2)}) %all-to-all-start.2) | async-done | bytes 524320 | tf_op jit(solution)/shard_map/all_to_all | solution.py:203
  83.6 1.3 %convolution_convert_fusion = bf16[256,1024]{1,0:T(8,128)(2,1)} fusion(bf16[256,1024]{1,0:T(8,128)(2,1)S(1)} %bitcast.17, s32[256]{0:T(256)S(1)} %add.22, s32[256]{0:T(256)S(1)} %get-tuple-element.6, s32[256]{0:T(256)S(1)} %get-tuple-element.7, pred[256]{0:T(512)(128)(4,1)S(1)} %compare_and_fusion), kind=kOutput, calls=%fused_computation | convolution fusion | flops 134742016 | bytes 1051904 | tf_op jit(solution)/shard_map/dot_general | solution.py:206
  (2 shorter events, 0.0 us)
Async XLA Ops:
  0.6 15.4 %copy-start = (bf16[8,32,1024]{2,1,0:T(8,128)(2,1)S(1)}, bf16[8,32,1024]{2,1,0:T(8,128)(2,1)}, u32[]{:S(2)}) copy-start(bf16[8,32,1024]{2,1,0:T(8,128)(2,1)} %param.10) | copy-start | bytes 1572868
  0.6 20.1 %copy-start.2 = (bf16[100,1024]{1,0:T(8,128)(2,1)S(1)}, bf16[100,1024]{1,0:T(8,128)(2,1)}, u32[]{:S(2)}) copy-start(bf16[100,1024]{1,0:T(8,128)(2,1)} %param.13) | copy-start | bytes 614404
  0.7 20.9 %copy-start.3 = (f32[100,128]{1,0:T(8,128)S(1)}, f32[100,128]{1,0:T(8,128)}, u32[]{:S(2)}) copy-start(f32[100,128]{1,0:T(8,128)} %param.14) | copy-start | bytes 153604
  2.1 13.7 %all-to-all-start = ((s32[16,1,2]{2,1,0:T(1,128)}), s32[16,1,2]{2,1,0:T(1,128)S(1)}, u32[]{:S(2)}, u32[]{:S(2)}) async-start(s32[16,1,2]{2,1,0:T(1,128)} %copy.19), calls=%async_computation | async-start | bytes 16384 | tf_op jit(solution)/shard_map/all_to_all | solution.py:187
  17.2 18.0 %all-to-all-start.1 = ((bf16[16,16,1024]{2,1,0:T(8,128)(2,1)}), bf16[16,16,1024]{2,1,0:T(8,128)(2,1)S(1)}, u32[]{:S(2)}, u32[]{:S(2)}) async-start(bf16[16,16,1024]{2,1,0:T(8,128)(2,1)} %bitcast.4), calls=%async_computation.1 | async-start | bytes 1048576 | tf_op jit(solution)/shard_map/all_to_all | solution.py:194
  35.2 0.8 copy-start.1
  65.6 18.0 %all-to-all-start.2 = ((bf16[16,16,1024]{2,1,0:T(8,128)(2,1)}), bf16[16,16,1024]{2,1,0:T(8,128)(2,1)S(1)}, u32[]{:S(2)}, u32[]{:S(2)}) async-start(bf16[16,16,1024]{2,1,0:T(8,128)(2,1)} %bitcast.18), calls=%async_computation.2 | async-start | bytes 1048576 | tf_op jit(solution)/shard_map/all_to_all | solution.py:203
where the time goes:
time: 86.5 us; the launch traced here: 86 us
  waiting for transfers between devices  32.5 us (38%)
  Pallas kernels  17.4 us (20%)
  starting transfers between devices  14.5 us (17%)
  blocking collectives  10.2 us (12%)
  local copies, waits for them, and re-layouts  4.41 us (5%)
  matrix products  2.51 us (3%)
  between operations  2.51 us (3%)
  other arithmetic  1.88 us (2%)
    pallas_call x1, Pallas kernels, decode(): pl.pallas_call(functools.partial(decoder_kernel, members, fields, slots,...  17.4 us
    all_to_all x1, waiting for transfers between devices, local(): lax.all_to_all(grads.reshape(shards, per, width), 'space', split_axis=0,...  13.2 us
    all_to_all x1, waiting for transfers between devices, local(): lax.all_to_all(picked.reshape(shards, per, width), 'space', split_axis=0,...  13.1 us
    all_to_all x1, blocking collectives, local(): lax.all_to_all(jnp.broadcast_to(jnp.sum(total), (shards, 128)), 'space',...  10.2 us
    all_to_all x1, starting transfers between devices, local(): lax.all_to_all(request.reshape(shards, cap), 'space', split_axis=0, conca...  7.39 us
    all_to_all x1, waiting for transfers between devices, local(): lax.all_to_all(request.reshape(shards, cap), 'space', split_axis=0, conca...  6.31 us
    all_to_all x1, starting transfers between devices, local(): lax.all_to_all(picked.reshape(shards, per, width), 'space', split_axis=0,...  3.57 us
    all_to_all x1, starting transfers between devices, local(): lax.all_to_all(grads.reshape(shards, per, width), 'space', split_axis=0,...  3.57 us
  transfers between devices with their start and end apart: 3, of which 3 were waited for; matrix products, arithmetic and copies ran while one was open for 2% of the time, Pallas kernels for 0%

commit v1 on v0

--- a/solution.py
+++ b/solution.py
@@ -31,12 +31,12 @@
 
 def decoder_kernel(
     members, fields, slots, cap,
-    x_ref, lat_ref, qw_ref, kvw_ref, fw_ref, target_ref, area_ref, edge_ref,
+    q_s, lat_ref, kvw_ref, fw_ref, target_ref, area_ref, edge_ref,
     out_ref, total_ref,
-    q_s, kv_s, p_s, att_s, pred_s, dp_s, da_s, sg_s,
+    kv_s, p_s, att_s, pred_s, dp_s, da_s, sg_s,
 ):
     points = target_ref.shape[1]
-    width = qw_ref.shape[0]
+    width = kvw_ref.shape[0]
     rows = members * slots
     head_dim = width // HEADS
     group_heads = 256 // head_dim
@@ -45,8 +45,6 @@
     latent = dot(order, lat_ref[...], (1, 0)).astype(BF)
     for c in range(0, 2 * width, 512):
         kv_s[:, c:c + 512] = dot(latent, kvw_ref[:, c:c + 512], (1, 0)).astype(BF)
-    for c in range(0, width, 256):
-        q_s[:, c:c + 256] = dot(x_ref[...], qw_ref[:, c:c + 256], (1, 0)).astype(BF)
 
     hs = group_heads * slots
     head_mask = (iota((hs, 256), 0) // slots == iota((hs, 256), 1) // head_dim).astype(F32)
@@ -146,8 +144,8 @@
     out_ref[...] = dot(order, latent_grad, (0, 0)).astype(BF)
 
 
-def decode(grid_latent, latent, query_weight, kv_weight, field_weight, target, area, edge_slot, members, slots, cap, fields):
-    points, width = target.shape[1], query_weight.shape[0]
+def decode(queries, latent, kv_weight, field_weight, target, area, edge_slot, members, slots, cap, fields):
+    points, width = target.shape[1], kv_weight.shape[0]
     padded = field_weight.shape[0]
     rows = members * slots
     group_heads = 256 * HEADS // width
@@ -158,10 +156,9 @@
             jax.ShapeDtypeStruct((rows, width), BF),
             jax.ShapeDtypeStruct((8, points), F32),
         ),
-        in_specs=[vmem] * 8,
+        in_specs=[vmem] * 7,
         out_specs=(vmem, vmem),
         scratch_shapes=[
-            pltpu.VMEM((members * points, width), BF),
             pltpu.VMEM((rows, 2 * width), BF),
             pltpu.VMEM((members, HEADS // group_heads, group_heads * slots, points), F32),
             pltpu.VMEM((width, members * points), BF),
@@ -171,7 +168,153 @@
             pltpu.VMEM((rows, 2 * width), BF),
         ],
         compiler_params=pltpu.CompilerParams(vmem_limit_bytes=56 * 1024 * 1024),
-    )(grid_latent, latent, query_weight, kv_weight, field_weight, target, area, edge_slot)
+    )(queries, latent, kv_weight, field_weight, target, area, edge_slot)
+
+
+def greet(shards, me):
+    barrier = pltpu.get_barrier_semaphore()
+
+    def tell(step, carry):
+        partner = lax.rem(me + step, shards)
+        pl.semaphore_signal(barrier, inc=1, device_id={"space": partner}, device_id_type=pl.DeviceIdType.MESH)
+        return carry
+
+    lax.fori_loop(1, shards, tell, 0)
+    pl.semaphore_wait(barrier, shards - 1)
+
+
+def part(index, size):
+    return pl.ds(pl.multiple_of(index * size, size), size)
+
+
+def exchange(shards, me, size, src, dst, send_sem, recv_sem, whole=False):
+    def copy(partner, landing):
+        return pltpu.make_async_remote_copy(
+            src_ref=src if whole else src.at[part(partner, size)],
+            dst_ref=dst.at[part(landing, size)],
+            send_sem=send_sem.at[partner],
+            recv_sem=recv_sem.at[landing],
+            device_id={"space": partner},
+            device_id_type=pl.DeviceIdType.MESH,
+        )
+
+    def start(step, carry):
+        copy(lax.rem(me + step, shards), me).start()
+        return carry
+
+    def finish(step, carry):
+        copy(lax.rem(me + step, shards), me).wait_send()
+        sender = lax.rem(me + shards - step, shards)
+        copy(sender, sender).wait_recv()
+        return carry
+
+    lax.fori_loop(1, shards, start, 0)
+    return lambda: lax.fori_loop(1, shards, finish, 0)
+
+
+def selection(got, members, nodes):
+    member = iota(got.shape, 0) % members
+    lane = iota(got.shape, 1)
+    parts = [
+        (lane + c == member * nodes + got).astype(F32).astype(BF)
+        for c in range(0, members * nodes, 128)
+    ]
+    return jnp.concatenate(parts, axis=1)
+
+
+def gather_kernel(
+    shards, members, nodes,
+    ask_ref, mesh_ref, x_ref, qw_ref, got_ref, q_ref, arrived_ref,
+    got_s, picked_s, arrived_s, ask_send, ask_recv, row_send, row_recv,
+):
+    me = lax.axis_index("space")
+    per = ask_ref.shape[0] // shards
+    width = mesh_ref.shape[1]
+
+    def project(first, last):
+        for c in range(first, last, 256):
+            q_ref[:, c:c + 256] = dot(x_ref[...], qw_ref[:, c:c + 256], (1, 0)).astype(BF)
+
+    greet(shards, me)
+    finish = exchange(shards, me, per, ask_ref, got_s, ask_send, ask_recv)
+    got_s[part(me, per), :] = ask_ref[part(me, per), :]
+    project(0, width // 2)
+    finish()
+    got = got_s[...]
+    got_ref[...] = got
+    picked_s[...] = dot(selection(got, members, nodes), mesh_ref[...], (1, 0)).astype(BF)
+    finish = exchange(shards, me, per, picked_s, arrived_s, row_send, row_recv)
+    arrived_s[part(me, per), :] = picked_s[part(me, per), :]
+    project(width // 2, width)
+    finish()
+    arrived_ref[...] = arrived_s[...]
+
+
+def gather_rows(ask, mesh_rows, x, query_weight, shards, members, nodes):
+    rows, width = ask.shape[0], mesh_rows.shape[1]
+    vmem = pl.BlockSpec(memory_space=pltpu.VMEM)
+    sems = pltpu.SemaphoreType.DMA((shards,))
+    return pl.pallas_call(
+        functools.partial(gather_kernel, shards, members, nodes),
+        out_shape=(
+            jax.ShapeDtypeStruct(ask.shape, jnp.int32),
+            jax.ShapeDtypeStruct(x.shape, BF),
+            jax.ShapeDtypeStruct((rows, width), BF),
+        ),
+        in_specs=[vmem] * 4,
+        out_specs=(vmem, vmem, vmem),
+        scratch_shapes=[
+            pltpu.VMEM(ask.shape, jnp.int32),
+            pltpu.VMEM((rows, width), BF),
+            pltpu.VMEM((rows, width), BF),
+            sems, sems, sems, sems,
+        ],
+        compiler_params=pltpu.CompilerParams(
+            collective_id=0, has_side_effects=True, vmem_limit_bytes=40 * 1024 * 1024
+        ),
+    )(ask, mesh_rows, x, query_weight)
+
+
+def return_kernel(
+    shards, members, nodes, count,
+    got_ref, grads_ref, total_ref, out_ref, loss_ref,
+    back_s, totals_s, row_send, row_recv, total_send, total_recv,
+):
+    me = lax.axis_index("space")
+    per = grads_ref.shape[0] // shards
+    greet(shards, me)
+    finish = exchange(shards, me, per, grads_ref, back_s, row_send, row_recv)
+    finish_total = exchange(shards, me, 8, total_ref, totals_s, total_send, total_recv, whole=True)
+    back_s[part(me, per), :] = grads_ref[part(me, per), :]
+    totals_s[part(me, 8), :] = total_ref[...]
+    select = selection(got_ref[...], members, nodes)
+    finish()
+    finish_total()
+    out_ref[...] = dot(select, back_s[...], (0, 0)).astype(BF)
+    loss_ref[...] = jnp.full(loss_ref.shape, 1.0, F32) * (jnp.sum(totals_s[...]) / count)
+
+
+def return_rows(got, grads, total, shards, members, nodes, count):
+    rows, width = grads.shape
+    vmem = pl.BlockSpec(memory_space=pltpu.VMEM)
+    sems = pltpu.SemaphoreType.DMA((shards,))
+    return pl.pallas_call(
+        functools.partial(return_kernel, shards, members, nodes, count),
+        out_shape=(
+            jax.ShapeDtypeStruct((members * nodes, width), BF),
+            jax.ShapeDtypeStruct((8, 128), F32),
+        ),
+        in_specs=[vmem] * 3,
+        out_specs=(vmem, vmem),
+        scratch_shapes=[
+            pltpu.VMEM((rows, width), BF),
+            pltpu.VMEM((shards * 8, total.shape[1]), F32),
+            sems, sems, sems, sems,
+        ],
+        compiler_params=pltpu.CompilerParams(
+            collective_id=1, has_side_effects=True, vmem_limit_bytes=40 * 1024 * 1024
+        ),
+    )(got, grads, total)
 
 
 def local(
@@ -184,32 +327,24 @@
     slots = shards * cap
     per = cap * members
     fields = target.shape[0]
-    incoming = lax.all_to_all(request.reshape(shards, cap), "space", split_axis=0, concat_axis=0, tiled=True)
-    wanted = jnp.broadcast_to(incoming[:, :, None], (shards, cap, members)).reshape(shards * per, 1)
-    member_of = iota((shards * per, members * nodes), 0) % members
-    column = iota((shards * per, members * nodes), 1)
-    select = (column == member_of * nodes + wanted).astype(BF)
-    rows = mesh_latent.reshape(members * nodes, width)
-    picked = jnp.dot(select, rows, preferred_element_type=F32).astype(BF)
-    arrived = lax.all_to_all(
-        picked.reshape(shards, per, width), "space", split_axis=0, concat_axis=0, tiled=True
-    ).reshape(shards * per, width)
+    ask = jnp.broadcast_to(
+        request.reshape(slots, 1, 1), (slots, members, 128)
+    ).reshape(shards * per, 128)
+    got, queries, arrived = gather_rows(
+        ask, mesh_latent.reshape(members * nodes, width), grid_latent.reshape(members * points, width),
+        query_weight, shards, members, nodes,
+    )
     field_pad = jnp.pad(field_weight, ((0, 128 - fields), (0, 0)))
     target_pad = jnp.pad(target, ((0, -fields % 8), (0, 0)))
     grads, total = decode(
-        grid_latent.reshape(members * points, width), arrived, query_weight, kv_weight, field_pad,
-        target_pad, area_weight.reshape(1, points), edge_slot, members, slots, cap, fields,
-    )
-    returned = lax.all_to_all(
-        grads.reshape(shards, per, width), "space", split_axis=0, concat_axis=0, tiled=True
-    ).reshape(shards * per, width)
-    mesh_grad = lax.dot_general(
-        select, returned, (((0,), (0,)), ((), ())), preferred_element_type=F32
-    ).astype(BF).reshape(members, nodes, width)
-    totals = lax.all_to_all(
-        jnp.broadcast_to(jnp.sum(total), (shards, 128)), "space", split_axis=0, concat_axis=0, tiled=True
-    )
-    mean_loss = (jnp.sum(totals[:, 0]) / (fields * points * shards)).reshape(1)
+        queries, arrived, kv_weight, field_pad, target_pad, area_weight.reshape(1, points), edge_slot,
+        members, slots, cap, fields,
+    )
+    mesh_grad, loss = return_rows(
+        got, grads, total, shards, members, nodes, float(fields * points * shards)
+    )
+    mesh_grad = mesh_grad.reshape(members, nodes, width)
+    mean_loss = loss[0, 0:1]
     return (mesh_grad, mean_loss)
 
 

time: 86.5 us -> 71.2 us (0.82)
  Pallas kernels: 17.4 us -> 56.5 us
  waiting for transfers between devices: 32.5 us -> 0 us
  starting transfers between devices: 14.5 us -> 0 us
  blocking collectives: 10.2 us -> 0 us
  local copies, waits for them, and re-layouts: 4.41 us -> 13.6 us
  matrix products: 2.51 us -> 0 us
  other arithmetic: 1.88 us -> 0 us
  between operations: 2.51 us -> 0.68 us
    pallas_call x0 -> x2, Pallas kernels: none -> 41.8 us  [the longest x1 21 us: gather_rows(): pl.pallas_call(functools.partial(gather_kernel, shards, members, nodes),...]
    all_to_all x3 -> x0, waiting for transfers between devices: 32.5 us -> none  [the longest x1 13.2 us: local(): lax.all_to_all(grads.reshape(shards, per, width), 'space', split_axis=0,...]
    all_to_all x3 -> x0, starting transfers between devices: 14.5 us -> none  [the longest x1 7.39 us: local(): lax.all_to_all(request.reshape(shards, cap), 'space', split_axis=0, conca...]
    all_to_all x1 -> x0, blocking collectives: 10.2 us -> none  [local(): lax.all_to_all(jnp.broadcast_to(jnp.sum(total), (shards, 128)), 'space',...]
    unnamed x8 -> x16, local copies, waits for them, and re-layouts: 0.81 us -> 9.61 us
    pallas_call x1, Pallas kernels: 17.4 us -> 14.7 us  [decode(): pl.pallas_call(functools.partial(decoder_kernel, members, fields, slots,...]
    dot_general x2 -> x0, matrix products: 2.51 us -> none  [the longest x1 1.31 us: local(): lax.dot_general(select, returned, (((0,), (0,)), ((), ())), preferred_ele...]
    reduce_sum x2 -> x0, other arithmetic: 1.88 us -> none  [the longest x1 1.28 us: local(): jnp.sum(total)]
  transfers between devices with their start and end apart: 3 -> 0, of which waited for: 3 -> 0; matrix products, arithmetic and copies ran while one was open for 2% -> 0% of each run, Pallas kernels for 0% -> 0%
where the time goes in v1:
time: 71.2 us; the launch traced here: 70.8 us
  Pallas kernels  56.5 us (79%)
  local copies, waits for them, and re-layouts  13.6 us (19%)
    pallas_call x1, Pallas kernels, gather_rows(): pl.pallas_call(functools.partial(gather_kernel, shards, members, nodes),...  21 us
    pallas_call x1, Pallas kernels, return_rows(): pl.pallas_call(functools.partial(return_kernel, shards, members, nodes, c...  20.8 us
    pallas_call x1, Pallas kernels, decode(): pl.pallas_call(functools.partial(decoder_kernel, members, fields, slots,...  14.7 us
    unnamed x16, local copies, waits for them, and re-layouts  9.61 us
    pad x1, local copies, waits for them, and re-layouts, local(): field_pad = jnp.pad(field_weight, ((0, 128 - fields), (0, 0)))  1.67 us
    pad x1, local copies, waits for them, and re-layouts, local(): target_pad = jnp.pad(target, ((0, -fields % 8), (0, 0)))  1.44 us

profile of v1, /device:TPU:0, one launch (start us, length us, event | category | flops | bytes accessed | tf_op | source)
XLA Modules:
  0.0 70.8 jit_solution(8482648559160626717)
XLA Ops:
  0.6 0.8 %copy.12 = s32[1,16,2]{2,1,0:T(8,128)S(1)} copy(s32[1,16,2]{1,2,0:T(2,128)} %param.16) | data formatting | bytes 256 | tf_op args[7]
  1.4 0.1 broadcast_in_dim.11
  1.5 0.1 broadcast_in_dim.12
  1.5 0.1 broadcast_in_dim.13
  1.6 1.4 %pad.9.target_ref = f32[104,128]{1,0:T(8,128)} pad(f32[100,128]{1,0:T(8,128)} %param.14, f32[]{:T(128)} %constant.4.clone.1), padding=0_4x0_0 | pad | bytes 104452 | tf_op jit(solution)/shard_map/jit(_pad)/pad | solution.py:338
  3.1 0.1 broadcast_in_dim.14.ask_ref
  3.2 1.7 %pad.8.fw_ref = bf16[128,1024]{1,0:T(8,128)(2,1)} pad(bf16[100,1024]{1,0:T(8,128)(2,1)} %param.13, bf16[]{:T(256)} %constant.3.clone.1), padding=0_28x0_0 | pad | bytes 466946 | tf_op jit(solution)/shard_map/jit(_pad)/pad | solution.py:337
  4.8 0.0 copy-start
  4.8 1.6 %copy-done = bf16[8,128,1024]{2,1,0:T(8,128)(2,1)S(1)} copy-done((bf16[8,128,1024]{2,1,0:T(8,128)(2,1)S(1)}, bf16[8,128,1024]{2,1,0:T(8,128)(2,1)}, u32[]{:S(2)}) %copy-start) | copy-done | bytes 2097176
  6.4 0.0 copy-start.1
  6.4 1.6 %copy-done.1 = bf16[1024,1024]{1,0:T(8,128)(2,1)S(1)} copy-done((bf16[1024,1024]{1,0:T(8,128)(2,1)S(1)}, bf16[1024,1024]{1,0:T(8,128)(2,1)}, u32[]{:S(2)}) %copy-start.1) | copy-done | bytes 2097176
  8.0 0.0 copy-start.3
  8.0 1.0 %copy-done.3 = bf16[8,32,1024]{2,1,0:T(8,128)(2,1)S(1)} copy-done((bf16[8,32,1024]{2,1,0:T(8,128)(2,1)S(1)}, bf16[8,32,1024]{2,1,0:T(8,128)(2,1)}, u32[]{:S(2)}) %copy-start.3) | copy-done | bytes 524312
  9.1 21.0 %shard_map.104 = (s32[256,128]{1,0:T(8,128)S(1)}, bf16[1024,1024]{1,0:T(8,128)(2,1)S(1)}, bf16[256,1024]{1,0:T(8,128)(2,1)S(1)}) custom-call(s32[256,128]{1,0:T(8,128)S(1)} %broadcast_in_dim.14.ask_ref, bf16[256,1024]{1,0:T(8,128)(2,1)S(1)} %bitcast.6, bf16[1024,1024]{1,0:T(8,128)(2,1)S(1)} %bitcast.5, bf16[1024,1024]{1,0:T(8,128)(2,1)S(1)} %copy-done.1), custom_call_target="tpu_custom_call" | custom-call | tf_op jit(solution)/shard_map/pallas_call | solution.py:257
  30.1 0.0 copy-start.2
  30.1 1.3 %copy-done.2 = bf16[1024,1024]{1,0:T(8,128)(2,1)} copy-done((bf16[1024,1024]{1,0:T(8,128)(2,1)}, bf16[1024,1024]{1,0:T(8,128)(2,1)S(1)}, u32[]{:S(2)}) %copy-start.2) | copy-done | bytes 2097176
  31.4 0.0 copy-start.5
  31.4 0.8 %copy-done.5 = bf16[256,1024]{1,0:T(8,128)(2,1)} copy-done((bf16[256,1024]{1,0:T(8,128)(2,1)}, bf16[256,1024]{1,0:T(8,128)(2,1)S(1)}, u32[]{:S(2)}) %copy-start.5) | copy-done | bytes 524312
  32.2 14.7 %shard_map.105 = (bf16[256,1024]{1,0:T(8,128)(2,1)}, f32[8,128]{1,0:T(8,128)}) custom-call(bf16[1024,1024]{1,0:T(8,128)(2,1)} %copy-done.2, bf16[256,1024]{1,0:T(8,128)(2,1)} %copy-done.5, bf16[1024,2048]{1,0:T(8,128)(2,1)} %kvw_ref.1, bf16[128,1024]{1,0:T(8,128)(2,1)} %pad.8.fw_ref, f32[104,128]{1,0:T(8,128)} %pad.9.target_ref, f32[1,128]{1,0:T(1,128)} %bitcast.8, ...), custom_call_target="tpu_custom_call" | custom-call | tf_op jit(solution)/shard_map/pallas_call | solution.py:153
  46.9 0.0 copy-start.4
  46.9 1.0 %copy-done.4 = bf16[256,1024]{1,0:T(8,128)(2,1)S(1)} copy-done((bf16[256,1024]{1,0:T(8,128)(2,1)S(1)}, bf16[256,1024]{1,0:T(8,128)(2,1)}, u32[]{:S(2)}) %copy-start.4) | copy-done | bytes 524312
  48.0 0.0 copy-start.6
  48.0 0.7 copy-done.6
  48.6 20.8 %shard_map.106 = (bf16[256,1024]{1,0:T(8,128)(2,1)S(1)}, f32[8,128]{1,0:T(8,128)S(1)}) custom-call(s32[256,128]{1,0:T(8,128)S(1)} %get-tuple-element.9.got_ref, bf16[256,1024]{1,0:T(8,128)(2,1)S(1)} %copy-done.4, f32[8,128]{1,0:T(8,128)S(1)} %copy-done.6), custom_call_target="tpu_custom_call" | custom-call | tf_op jit(solution)/shard_map/pallas_call | solution.py:301
  69.5 0.5 slice.3
  70.0 0.8 %copy.14 = bf16[8,32,1024]{2,1,0:T(8,128)(2,1)} copy(bf16[8,32,1024]{2,1,0:T(8,128)(2,1)S(1)} %bitcast.7) | data formatting | bytes 1048576
Async XLA Ops:
  4.8 1.6 %copy-start = (bf16[8,128,1024]{2,1,0:T(8,128)(2,1)S(1)}, bf16[8,128,1024]{2,1,0:T(8,128)(2,1)}, u32[]{:S(2)}) copy-start(bf16[8,128,1024]{2,1,0:T(8,128)(2,1)} %param.9) | copy-start | bytes 6291460
  6.4 1.6 %copy-start.1 = (bf16[1024,1024]{1,0:T(8,128)(2,1)S(1)}, bf16[1024,1024]{1,0:T(8,128)(2,1)}, u32[]{:S(2)}) copy-start(bf16[1024,1024]{1,0:T(8,128)(2,1)} %qw_ref.1) | copy-start | bytes 6291460
  8.0 1.0 %copy-start.3 = (bf16[8,32,1024]{2,1,0:T(8,128)(2,1)S(1)}, bf16[8,32,1024]{2,1,0:T(8,128)(2,1)}, u32[]{:S(2)}) copy-start(bf16[8,32,1024]{2,1,0:T(8,128)(2,1)} %param.10) | copy-start | bytes 1572868
  30.1 1.3 %copy-start.2 = (bf16[1024,1024]{1,0:T(8,128)(2,1)}, bf16[1024,1024]{1,0:T(8,128)(2,1)S(1)}, u32[]{:S(2)}) copy-start(bf16[1024,1024]{1,0:T(8,128)(2,1)S(1)} %get-tuple-element.10.q_s) | copy-start | bytes 6291460
  31.4 0.8 %copy-start.5 = (bf16[256,1024]{1,0:T(8,128)(2,1)}, bf16[256,1024]{1,0:T(8,128)(2,1)S(1)}, u32[]{:S(2)}) copy-start(bf16[256,1024]{1,0:T(8,128)(2,1)S(1)} %get-tuple-element.11.lat_ref) | copy-start | bytes 1572868
  46.9 1.0 %copy-start.4 = (bf16[256,1024]{1,0:T(8,128)(2,1)S(1)}, bf16[256,1024]{1,0:T(8,128)(2,1)}, u32[]{:S(2)}) copy-start(bf16[256,1024]{1,0:T(8,128)(2,1)} %get-tuple-element.12.grads_ref) | copy-start | bytes 1572868
  48.0 0.7 copy-start.6

commit v2 on v0

v2 whole, which is shorter than its diff:
```python
import functools
import math

import jax
import jax.numpy as jnp
from jax import lax
from jax.experimental import pallas as pl
from jax.experimental.pallas import tpu as pltpu
from jax.sharding import PartitionSpec as P

HEADS = 16
SMOOTHING = 0.04
FAIRNESS = 0.95
BF = jnp.bfloat16
F32 = jnp.float32


def dot(a, b, dims):
    return lax.dot_general(a, b, ((dims[:1], dims[1:]), ((), ())), preferred_element_type=F32)


def iota(shape, dim):
    return lax.broadcasted_iota(jnp.int32, shape, dim)


def order_matrix(rows, members, slots, cap):
    r, c = iota((rows, rows), 0), iota((rows, rows), 1)
    member, slot = r // slots, r % slots
    return (c == slot * members + member).astype(F32).astype(BF)


def greet(shards, me):
    barrier = pltpu.get_barrier_semaphore()

    def tell(step, carry):
        partner = lax.rem(me + step, shards)
        pl.semaphore_signal(barrier, inc=1, device_id={"space": partner}, device_id_type=pl.DeviceIdType.MESH)
        return carry

    lax.fori_loop(1, shards, tell, 0)
    pl.semaphore_wait(barrier, shards - 1)


def part(index, size):
    return pl.ds(pl.multiple_of(index * size, size), size)


def exchange(shards, me, size, src, dst, send_sem, recv_sem, whole=False):
    def copy(partner, landing):
        return pltpu.make_async_remote_copy(
            src_ref=src if whole else src.at[part(partner, size)],
            dst_ref=dst.at[part(landing, size)],
            send_sem=send_sem.at[partner],
            recv_sem=recv_sem.at[landing],
            device_id={"space": partner},
            device_id_type=pl.DeviceIdType.MESH,
        )

    def start(step, carry):
        copy(lax.rem(me + step, shards), me).start()
        return carry

    def finish(step, carry):
        copy(lax.rem(me + step, shards), me).wait_send()
        sender = lax.rem(me + shards - step, shards)
        copy(sender, sender).wait_recv()
        return carry

    lax.fori_loop(1, shards, start, 0)
    return lambda: lax.fori_loop(1, shards, finish, 0)


def selection(got, members, nodes):
    member = iota(got.shape, 0) % members
    lane = iota(got.shape, 1)
    parts = [
        (lane + c == member * nodes + got).astype(F32).astype(BF)
        for c in range(0, members * nodes, 128)
    ]
    return jnp.concatenate(parts, axis=1)


def decoder_kernel(
    shards, members, fields, slots, cap, nodes, count,
    ask_ref, mesh_ref, fw_ref, target_ref, area_ref, edge_ref, x_hbm, qw_hbm, kvw_hbm,
    out_ref, loss_ref,
    x_s, qw_s, kvw_s, got_s, picked_s, arrived_s, grads_s, back_s, total_s, totals_s,
    q_s, kv_s, p_s, att_s, target_s, pred_s, dp_s, da_s, sg_s,
    ask_send, ask_recv, row_send, row_recv, back_send, back_recv, total_send, total_recv, load_sem,
):
    me = lax.axis_index("space")
    points = target_ref.shape[1]
    width = mesh_ref.shape[1]
    rows = members * slots
    per = cap * members
    head_dim = width // HEADS
    group_heads = 256 // head_dim
    groups = HEADS // group_heads
    hs = group_heads * slots
    padded = pred_s.shape[0]

    loads = [
        pltpu.make_async_copy(src, dst, load_sem.at[i])
        for i, (src, dst) in enumerate(((x_hbm, x_s), (qw_hbm, qw_s), (kvw_hbm, kvw_s)))
    ]
    for load in loads:
        load.start()

    greet(shards, me)
    finish = exchange(shards, me, per, ask_ref, got_s, ask_send, ask_recv)
    got_s[part(me, per), :] = ask_ref[part(me, per), :]
    target_s[...] = jnp.zeros(target_s.shape, F32)
    target_s[0:fields, :] = target_ref[...]
    finish()
    select = selection(got_s[...], members, nodes)
    picked_s[...] = dot(select, mesh_ref[...], (1, 0)).astype(BF)
    finish = exchange(shards, me, per, picked_s, arrived_s, row_send, row_recv)
    arrived_s[part(me, per), :] = picked_s[part(me, per), :]
    loads[0].wait()
    loads[1].wait()
    for c in range(0, width, 256):
        q_s[:, c:c + 256] = dot(x_s[...], qw_s[:, c:c + 256], (1, 0)).astype(BF)
    order = order_matrix(rows, members, slots, cap)
    head_mask = (iota((hs, 256), 0) // slots == iota((hs, 256), 1) // head_dim).astype(F32)
    head_mask16 = head_mask.astype(BF)
    slot_ids = iota((slots, points), 0)
    named = (slot_ids == edge_ref[0:1, :]) | (slot_ids == edge_ref[1:2, :]) | (slot_ids == edge_ref[2:3, :])
    named = named.astype(F32)
    named = jnp.concatenate([named] * group_heads, axis=0) > 0.5
    loads[2].wait()
    finish()

    latent = dot(order, arrived_s[...], (1, 0)).astype(BF)
    for c in range(0, 2 * width, 512):
        kv_s[:, c:c + 512] = dot(latent, kvw_s[:, c:c + 512], (1, 0)).astype(BF)

    def blocks(values):
        return jnp.concatenate([values] * group_heads, axis=0) * head_mask16

    scale = 1.0 / math.sqrt(head_dim)

    def attend(e):
        rs, gs = part(e, slots), part(e, points)
        for k in range(groups):
            cs = slice(k * 256, (k + 1) * 256)
            keys = blocks(kv_s[rs, cs])
            values = blocks(kv_s[rs, width + k * 256:width + (k + 1) * 256])
            score = dot(keys, q_s[gs, cs], (1, 1)) * scale
            exponent = jnp.where(named, jnp.exp(score), 0.0)
            by_head = exponent.reshape(group_heads, slots, points)
            total = jnp.sum(by_head, axis=1, keepdims=True)
            weight = (by_head / total).reshape(hs, points)
            p_s[e, k] = weight
            att_s[cs, gs] = dot(values, weight.astype(BF), (0, 0)).astype(BF)

    def by_pairs(work):
        def step(i, carry):
            work(2 * i)
            work(2 * i + 1)
            return carry

        lax.fori_loop(0, members // 2, step, 0)

    by_pairs(attend)
    pred_s[0:fields, :] = dot(fw_ref[...], att_s[...], (1, 0))
    if padded > fields:
        pred_s[fields:padded, :] = jnp.zeros((padded - fields, members * points), F32)

    area = area_ref[...]
    almost_fair = 1.0 - (1.0 - FAIRNESS) / members
    spread_factor = almost_fair / (members * (members - 1))

    def judge(i, total):
        fs = part(i, 8)
        goal = target_s[fs, :]
        preds = [pred_s[fs, e * points:(e + 1) * points] for e in range(members)]
        slopes = []
        skill = jnp.zeros((8, points), F32)
        for e in range(members):
            u = preds[e] - goal
            v = u * u + SMOOTHING
            r = lax.rsqrt(v)
            skill += v * r
            slopes.append(u * r * (1.0 / members))
        spread = jnp.zeros((8, points), F32)
        pulls = [jnp.zeros((8, points), F32) for _ in range(members)]
        for a in range(members):
            for b in range(a + 1, members):
                u = preds[a] - preds[b]
                v = u * u + SMOOTHING
                r = lax.rsqrt(v)
                spread += v * r
                w = u * r
                pulls[a] = pulls[a] + w
                pulls[b] = pulls[b] - w
        pointwise = skill * (1.0 / members) - spread_factor * spread
        valid = iota((8, points), 0) + i * 8 < fields
        for e in range(members):
            dp_s[fs, e * points:(e + 1) * points] = (slopes[e] - spread_factor * pulls[e]) * area
        return total + jnp.where(valid, pointwise * area, 0.0)

    total_s[...] = lax.fori_loop(0, padded // 8, judge, jnp.zeros((8, points), F32))
    finish_total = exchange(shards, me, 8, total_s, totals_s, total_send, total_recv, whole=True)
    totals_s[part(me, 8), :] = total_s[...]

    dp = dp_s[0:fields, :].astype(BF)
    for k in range(groups):
        cs = slice(k * 256, (k + 1) * 256)
        da_s[cs, :] = dot(fw_ref[:, cs], dp, (0, 0)).astype(BF)

    def fold(product):
        kept = (product * head_mask).reshape(group_heads, slots, 256)
        return jnp.sum(kept, axis=0).astype(BF)

    def backward(e):
        rs, gs = part(e, slots), part(e, points)
        for k in range(groups):
            cs = slice(k * 256, (k + 1) * 256)
            vs = slice(width + k * 256, width + (k + 1) * 256)
            values = blocks(kv_s[rs, vs])
            weight = p_s[e, k]
            da = da_s[cs, gs]
            dw = dot(values, da, (1, 0))
            pull = (weight * dw).reshape(group_heads, slots, points)
            mean = jnp.sum(pull, axis=1, keepdims=True)
            ds = pull - weight.reshape(group_heads, slots, points) * mean
            ds = (ds.reshape(hs, points) * scale).astype(BF)
            sg_s[rs, cs] = fold(dot(ds, q_s[gs, cs], (1, 0)))
            sg_s[rs, vs] = fold(dot(weight.astype(BF), da, (1, 1)))

    by_pairs(backward)
    latent_grad = dot(sg_s[...], kvw_s[...], (1, 1)).astype(BF)
    grads_s[...] = dot(order, latent_grad, (0, 0)).astype(BF)
    finish = exchange(shards, me, per, grads_s, back_s, back_send, back_recv)
    back_s[part(me, per), :] = grads_s[part(me, per), :]
    finish_total()
    loss_ref[...] = jnp.full(loss_ref.shape, 1.0, F32) * (jnp.sum(totals_s[...]) / count)
    finish()
    out_ref[...] = dot(select, back_s[...], (0, 0)).astype(BF)


def decode(ask, mesh_rows, x, query_weight, kv_weight, field_weight, target, area, edge_slot, shards, members, cap):
    fields, points = target.shape
    width = mesh_rows.shape[1]
    nodes = mesh_rows.shape[0] // members
    slots = shards * cap
    rows = members * slots
    padded = -(-fields // 8) * 8
    group_heads = 256 * HEADS // width
    vmem = pl.BlockSpec(memory_space=pltpu.VMEM)
    hbm = pl.BlockSpec(memory_space=pl.ANY)
    sems = pltpu.SemaphoreType.DMA((shards,))
    count = float(fields * points * shards)
    return pl.pallas_call(
        functools.partial(decoder_kernel, shards, members, fields, slots, cap, nodes, count),
        out_shape=(
            jax.ShapeDtypeStruct(mesh_rows.shape, BF),
            jax.ShapeDtypeStruct((8, 128), F32),
        ),
        in_specs=[vmem] * 6 + [hbm] * 3,
        out_specs=(vmem, vmem),
        scratch_shapes=[
            pltpu.VMEM(x.shape, BF),
            pltpu.VMEM(query_weight.shape, BF),
            pltpu.VMEM(kv_weight.shape, BF),
            pltpu.VMEM(ask.shape, jnp.int32),
            pltpu.VMEM((rows, width), BF),
            pltpu.VMEM((rows, width), BF),
            pltpu.VMEM((rows, width), BF),
            pltpu.VMEM((rows, width), BF),
            pltpu.VMEM((8, points), F32),
            pltpu.VMEM((shards * 8, points), F32),
            pltpu.VMEM((members * points, width), BF),
            pltpu.VMEM((rows, 2 * width), BF),
            pltpu.VMEM((members, HEADS // group_heads, group_heads * slots, points), F32),
            pltpu.VMEM((width, members * points), BF),
            pltpu.VMEM((padded, points), F32),
            pltpu.VMEM((padded, members * points), F32),
            pltpu.VMEM((padded, members * points), F32),
            pltpu.VMEM((width, members * points), BF),
            pltpu.VMEM((rows, 2 * width), BF),
        ] + [sems] * 8 + [pltpu.SemaphoreType.DMA((3,))],
        compiler_params=pltpu.CompilerParams(
            collective_id=0, has_side_effects=True, vmem_limit_bytes=60 * 1024 * 1024
        ),
    )(ask, mesh_rows, field_weight, target, area, edge_slot, x, query_weight, kv_weight)


def local(
    grid_latent, mesh_latent, query_weight, kv_weight, field_weight, target, area_weight, request, edge_slot,
):
    members, points, width = grid_latent.shape
    nodes = mesh_latent.shape[1]
    shards = lax.axis_size("space")
    cap = request.shape[2]
    slots = shards * cap
    per = cap * members
    ask = jnp.broadcast_to(
        request.reshape(slots, 1, 1), (slots, members, 128)
    ).reshape(shards * per, 128)
    mesh_grad, loss = decode(
        ask, mesh_latent.reshape(members * nodes, width), grid_latent.reshape(members * points, width),
        query_weight, kv_weight, field_weight, target, area_weight.reshape(1, points), edge_slot,
        shards, members, cap,
    )
    mesh_grad = mesh_grad.reshape(members, nodes, width)
    mean_loss = loss[0, 0:1]
    return (mesh_grad, mean_loss)


def solution(mesh):
    placed = (
        P(None, ("groups", "space"), None),
        P(None, ("groups", "space"), None),
        P(),
        P(),
        P(),
        P(None, ("groups", "space")),
        P(("groups", "space")),
        P(("groups", "space"), None, None),
        P(None, ("groups", "space")),
    )
    return jax.shard_map(
        local,
        mesh=mesh,
        in_specs=placed,
        out_specs=(P(None, ("groups", "space"), None), P("groups")),
        check_vma=False,
    )
```

time: 86.5 us -> 57.4 us (0.66)
  the two profiles are of different devices: /device:TPU:0 before, /device:TPU:25 now
where the time goes in v2:
time: 57.4 us; the launch traced here: 57.2 us
  Pallas kernels  51.7 us (90%)
  local copies, waits for them, and re-layouts  4.82 us (8%)
  between operations  0.64 us (1%)
    pallas_call x1, Pallas kernels, decode(): pl.pallas_call(functools.partial(decoder_kernel, shards, members, fields,...  51.7 us
    unnamed x2, local copies, waits for them, and re-layouts  2.62 us
    slice x1, local copies, waits for them, and re-layouts, local(): mean_loss = loss[0, 0:1]  1.19 us

profile of v2, /device:TPU:25, one launch (start us, length us, event | category | flops | bytes accessed | tf_op | source)
XLA Modules:
  0.0 57.2 jit_solution(15690625656303061468)
XLA Ops:
  0.6 0.8 %copy.12 = s32[1,16,2]{2,1,0:T(8,128)S(1)} copy(s32[1,16,2]{1,2,0:T(2,128)} %param.16) | data formatting | bytes 256 | tf_op args[7]
  1.4 0.1 broadcast_in_dim.11
  1.5 0.1 broadcast_in_dim.12
  1.5 0.1 broadcast_in_dim.13
  1.6 0.8 %broadcast_in_dim.14.ask_ref = s32[256,128]{1,0:T(8,128)} broadcast(s32[256]{0:T(256)S(1)} %broadcast_in_dim.13), dimensions={0} | broadcast | bytes 132096 | tf_op jit(solution)/shard_map/broadcast_in_dim | solution.py:298
  2.4 51.7 %shard_map.104 = (bf16[256,1024]{1,0:T(8,128)(2,1)}, f32[8,128]{1,0:T(8,128)}) custom-call(s32[256,128]{1,0:T(8,128)} %broadcast_in_dim.14.ask_ref, bf16[256,1024]{1,0:T(8,128)(2,1)} %bitcast.6, bf16[100,1024]{1,0:T(8,128)(2,1)} %fw_ref.1, f32[100,128]{1,0:T(8,128)} %target_ref.1, f32[1,128]{1,0:T(1,128)} %bitcast.8, s32[3,128]{1,0:T(4,128)} %edge_ref.1, ...), custom_call_target="tpu_custom_call" | custom-call | tf_op jit(solution)/shard_map/pallas_call | solution.py:254
  54.1 1.2 %slice.3 = f32[1,1]{1,0:T(1,128)} slice(f32[8,128]{1,0:T(8,128)} %get-tuple-element.5), slice={[0:1], [0:1]} | slice | bytes 8 | tf_op jit(solution)/shard_map/slice | solution.py:307
  55.3 1.9 %copy.14 = bf16[8,32,1024]{2,1,0:T(8,128)(2,1)} copy(bf16[8,32,1024]{2,1,0:T(8,128)(2,1)} %bitcast.7) | data formatting | bytes 1048576

commit v3 on v2

--- a/solution.py
+++ b/solution.py
@@ -11,6 +11,7 @@
 HEADS = 16
 SMOOTHING = 0.04
 FAIRNESS = 0.95
+PIECES = 2
 BF = jnp.bfloat16
 F32 = jnp.float32
 
@@ -23,10 +24,12 @@
     return lax.broadcasted_iota(jnp.int32, shape, dim)
 
 
-def order_matrix(rows, members, slots, cap):
-    r, c = iota((rows, rows), 0), iota((rows, rows), 1)
+def order_matrix(piece_members, slots, cap, column_part):
+    rows, per = piece_members * slots, PIECES * cap * piece_members
+    r, c = iota((rows, rows * PIECES), 0), iota((rows, rows * PIECES), 1)
     member, slot = r // slots, r % slots
-    return (c == slot * members + member).astype(F32).astype(BF)
+    place = slot // cap * per + column_part * cap * piece_members + slot % cap * piece_members + member
+    return (c == place).astype(F32).astype(BF)
 
 
 def greet(shards, me):
@@ -45,13 +48,13 @@
     return pl.ds(pl.multiple_of(index * size, size), size)
 
 
-def exchange(shards, me, size, src, dst, send_sem, recv_sem, whole=False):
+def exchange(shards, me, size, src, dst, send_sem, recv_sem, base=0, whole=False):
     def copy(partner, landing):
         return pltpu.make_async_remote_copy(
             src_ref=src if whole else src.at[part(partner, size)],
             dst_ref=dst.at[part(landing, size)],
-            send_sem=send_sem.at[partner],
-            recv_sem=recv_sem.at[landing],
+            send_sem=send_sem.at[base + partner],
+            recv_sem=recv_sem.at[base + landing],
             device_id={"space": partner},
             device_id_type=pl.DeviceIdType.MESH,
         )
@@ -70,14 +73,17 @@
     return lambda: lax.fori_loop(1, shards, finish, 0)
 
 
-def selection(got, members, nodes):
-    member = iota(got.shape, 0) % members
+def selection(got, piece_members, nodes):
+    columns = piece_members * nodes
+    lanes = min(128, columns)
+    got = got[:, :lanes]
+    member = iota(got.shape, 0) % piece_members
     lane = iota(got.shape, 1)
     parts = [
-        (lane + c == member * nodes + got).astype(F32).astype(BF)
-        for c in range(0, members * nodes, 128)
+        (lane + c == member * nodes + got).astype(F32)
+        for c in range(0, columns, lanes)
     ]
-    return jnp.concatenate(parts, axis=1)
+    return parts[0] if len(parts) == 1 else jnp.concatenate(parts, axis=1)
 
 
 def decoder_kernel(
@@ -112,15 +118,32 @@
     target_s[...] = jnp.zeros(target_s.shape, F32)
     target_s[0:fields, :] = target_ref[...]
     finish()
-    select = selection(got_s[...], members, nodes)
-    picked_s[...] = dot(select, mesh_ref[...], (1, 0)).astype(BF)
-    finish = exchange(shards, me, per, picked_s, arrived_s, row_send, row_recv)
-    arrived_s[part(me, per), :] = picked_s[part(me, per), :]
+    piece_members = members // PIECES
+    piece_rows = piece_members * nodes
+    wire_rows = shards * per
+    wide = width // PIECES
+    select = selection(got_s[...], piece_members, nodes)
+    column_part = iota(select.shape, 0) % per // (cap * piece_members)
+    selects = [jnp.where(column_part == p, select, 0.0).astype(BF) for p in range(PIECES)]
+    finish_rows = []
+    for h in range(PIECES):
+        ws = slice(h * wire_rows, (h + 1) * wire_rows)
+        picked = jnp.zeros((wire_rows, wide), F32)
+        for p in range(PIECES):
+            source = mesh_ref[h * piece_rows:(h + 1) * piece_rows, p * wide:(p + 1) * wide]
+            picked += dot(selects[p], source, (1, 0))
+        picked_s[ws, :] = picked.astype(BF)
+        source, landing = picked_s.at[ws], arrived_s.at[ws]
+        finish_rows.append(exchange(
+            shards, me, per, source, landing, row_send, row_recv, base=h * shards
+        ))
+        own = part(me + h * shards, per)
+        arrived_s[own, :] = picked_s[own, :]
     loads[0].wait()
     loads[1].wait()
     for c in range(0, width, 256):
         q_s[:, c:c + 256] = dot(x_s[...], qw_s[:, c:c + 256], (1, 0)).astype(BF)
-    order = order_matrix(rows, members, slots, cap)
+    orders = [order_matrix(piece_members, slots, cap, p) for p in range(PIECES)]
     head_mask = (iota((hs, 256), 0) // slots == iota((hs, 256), 1) // head_dim).astype(F32)
     head_mask16 = head_mask.astype(BF)
     slot_ids = iota((slots, points), 0)
@@ -128,11 +151,6 @@
     named = named.astype(F32)
     named = jnp.concatenate([named] * group_heads, axis=0) > 0.5
     loads[2].wait()
-    finish()
-
-    latent = dot(order, arrived_s[...], (1, 0)).astype(BF)
-    for c in range(0, 2 * width, 512):
-        kv_s[:, c:c + 512] = dot(latent, kvw_s[:, c:c + 512], (1, 0)).astype(BF)
 
     def blocks(values):
         return jnp.concatenate([values] * group_heads, axis=0) * head_mask16
@@ -153,15 +171,30 @@
             p_s[e, k] = weight
             att_s[cs, gs] = dot(values, weight.astype(BF), (0, 0)).astype(BF)
 
-    def by_pairs(work):
+    def by_pairs(work, h):
+        first = h * piece_members
+        for e in range(0, piece_members % 2):
+            work(first + e)
+
         def step(i, carry):
-            work(2 * i)
-            work(2 * i + 1)
+            work(first + piece_members % 2 + 2 * i)
+            work(first + piece_members % 2 + 2 * i + 1)
             return carry
 
-        lax.fori_loop(0, members // 2, step, 0)
-
-    by_pairs(attend)
+        lax.fori_loop(0, piece_members // 2, step, 0)
+
+    kv_rows = piece_members * slots
+    for h in range(PIECES):
+        finish_rows[h]()
+        arrived = arrived_s[h * wire_rows:(h + 1) * wire_rows, :]
+        latent = jnp.concatenate(
+            [dot(orders[p], arrived, (1, 0)).astype(BF) for p in range(PIECES)], axis=1
+        )
+        for c in range(0, 2 * width, 512):
+            kv_s[h * kv_rows:(h + 1) * kv_rows, c:c + 512] = dot(
+                latent, kvw_s[:, c:c + 512], (1, 0)
+            ).astype(BF)
+        by_pairs(attend, h)
     pred_s[0:fields, :] = dot(fw_ref[...], att_s[...], (1, 0))
     if padded > fields:
         pred_s[fields:padded, :] = jnp.zeros((padded - fields, members * points), F32)
@@ -228,15 +261,29 @@
             sg_s[rs, cs] = fold(dot(ds, q_s[gs, cs], (1, 0)))
             sg_s[rs, vs] = fold(dot(weight.astype(BF), da, (1, 1)))
 
-    by_pairs(backward)
-    latent_grad = dot(sg_s[...], kvw_s[...], (1, 1)).astype(BF)
-    grads_s[...] = dot(order, latent_grad, (0, 0)).astype(BF)
-    finish = exchange(shards, me, per, grads_s, back_s, back_send, back_recv)
-    back_s[part(me, per), :] = grads_s[part(me, per), :]
+    finish_back = []
+    for h in range(PIECES):
+        by_pairs(backward, h)
+        ws = slice(h * wire_rows, (h + 1) * wire_rows)
+        latent_grad = dot(sg_s[h * kv_rows:(h + 1) * kv_rows, :], kvw_s[...], (1, 1)).astype(BF)
+        sent = jnp.zeros((wire_rows, wide), F32)
+        for p in range(PIECES):
+            sent += dot(orders[p], latent_grad[:, p * wide:(p + 1) * wide], (0, 0))
+        grads_s[ws, :] = sent.astype(BF)
+        finish_back.append(exchange(
+            shards, me, per, grads_s.at[ws], back_s.at[ws], back_send, back_recv, base=h * shards
+        ))
+        own = part(me + h * shards, per)
+        back_s[own, :] = grads_s[own, :]
     finish_total()
     loss_ref[...] = jnp.full(loss_ref.shape, 1.0, F32) * (jnp.sum(totals_s[...]) / count)
-    finish()
-    out_ref[...] = dot(select, back_s[...], (0, 0)).astype(BF)
+    for h in range(PIECES):
+        finish_back[h]()
+        back = back_s[h * wire_rows:(h + 1) * wire_rows, :]
+        for p in range(PIECES):
+            out_ref[h * piece_rows:(h + 1) * piece_rows, p * wide:(p + 1) * wide] = dot(
+                selects[p], back, (0, 0)
+            ).astype(BF)
 
 
 def decode(ask, mesh_rows, x, query_weight, kv_weight, field_weight, target, area, edge_slot, shards, members, cap):
@@ -250,6 +297,7 @@
     vmem = pl.BlockSpec(memory_space=pltpu.VMEM)
     hbm = pl.BlockSpec(memory_space=pl.ANY)
     sems = pltpu.SemaphoreType.DMA((shards,))
+    piece_sems = pltpu.SemaphoreType.DMA((PIECES * shards,))
     count = float(fields * points * shards)
     return pl.pallas_call(
         functools.partial(decoder_kernel, shards, members, fields, slots, cap, nodes, count),
@@ -264,10 +312,10 @@
             pltpu.VMEM(query_weight.shape, BF),
             pltpu.VMEM(kv_weight.shape, BF),
             pltpu.VMEM(ask.shape, jnp.int32),
-            pltpu.VMEM((rows, width), BF),
-            pltpu.VMEM((rows, width), BF),
-            pltpu.VMEM((rows, width), BF),
-            pltpu.VMEM((rows, width), BF),
+            pltpu.VMEM((PIECES * rows, width // PIECES), BF),
+            pltpu.VMEM((PIECES * rows, width // PIECES), BF),
+            pltpu.VMEM((PIECES * rows, width // PIECES), BF),
+            pltpu.VMEM((PIECES * rows, width // PIECES), BF),
             pltpu.VMEM((8, points), F32),
             pltpu.VMEM((shards * 8, points), F32),
             pltpu.VMEM((members * points, width), BF),
@@ -279,7 +327,7 @@
             pltpu.VMEM((padded, members * points), F32),
             pltpu.VMEM((width, members * points), BF),
             pltpu.VMEM((rows, 2 * width), BF),
-        ] + [sems] * 8 + [pltpu.SemaphoreType.DMA((3,))],
+        ] + [sems] * 2 + [piece_sems] * 4 + [sems] * 2 + [pltpu.SemaphoreType.DMA((3,))],
         compiler_params=pltpu.CompilerParams(
             collective_id=0, has_side_effects=True, vmem_limit_bytes=60 * 1024 * 1024
         ),
@@ -296,7 +344,7 @@
     slots = shards * cap
     per = cap * members
     ask = jnp.broadcast_to(
-        request.reshape(slots, 1, 1), (slots, members, 128)
+        request.reshape(shards, 1, cap, 1, 1), (shards, PIECES, cap, members // PIECES, 128)
     ).reshape(shards * per, 128)
     mesh_grad, loss = decode(
         ask, mesh_latent.reshape(members * nodes, width), grid_latent.reshape(members * points, width),

time: 57.4 us -> 53.7 us (0.936)
  the two profiles are of different devices: /device:TPU:25 before, /device:TPU:0 now
where the time goes in v3:
time: 53.7 us; the launch traced here: 52.8 us
  Pallas kernels  47.4 us (88%)
  local copies, waits for them, and re-layouts  4.76 us (9%)
  between operations  0.65 us (1%)
    pallas_call x1, Pallas kernels, decode(): pl.pallas_call(functools.partial(decoder_kernel, shards, members, fields,...  47.4 us
    unnamed x1, local copies, waits for them, and re-layouts  1.87 us
    broadcast_in_dim x4, local copies, waits for them, and re-layouts, local(): jnp.broadcast_to(request.reshape(shards, 1, cap, 1, 1), (shards, PIECES,...  1.71 us
    slice x1, local copies, waits for them, and re-layouts, local(): mean_loss = loss[0, 0:1]  1.19 us

profile of v3, /device:TPU:0, one launch (start us, length us, event | category | flops | bytes accessed | tf_op | source)
XLA Modules:
  0.0 52.8 jit_solution(12034637996043123287)
XLA Ops:
  0.6 0.8 %copy.12 = s32[16,2]{1,0:T(8,128)S(1)} copy(s32[16,2]{0,1:T(2,128)} %bitcast.9) | data formatting | bytes 256 | tf_op jit(solution)/shard_map/broadcast_in_dim | solution.py:346
  1.4 0.1 broadcast_in_dim.12
  1.5 0.1 broadcast_in_dim.13
  1.6 0.8 %broadcast_in_dim.14.ask_ref = s32[256,128]{1,0:T(8,128)} broadcast(s32[256]{0:T(256)S(1)} %broadcast_in_dim.13), dimensions={0} | broadcast | bytes 132096 | tf_op jit(solution)/shard_map/broadcast_in_dim | solution.py:346
  2.4 47.4 %shard_map.104 = (bf16[256,1024]{1,0:T(8,128)(2,1)}, f32[8,128]{1,0:T(8,128)}) custom-call(s32[256,128]{1,0:T(8,128)} %broadcast_in_dim.14.ask_ref, bf16[256,1024]{1,0:T(8,128)(2,1)} %bitcast.7, bf16[100,1024]{1,0:T(8,128)(2,1)} %fw_ref.1, f32[100,128]{1,0:T(8,128)} %target_ref.1, f32[1,128]{1,0:T(1,128)} %bitcast.10, s32[3,128]{1,0:T(4,128)} %edge_ref.1, ...), custom_call_target="tpu_custom_call" | custom-call | tf_op jit(solution)/shard_map/pallas_call | solution.py:302
  49.8 1.2 %slice.3 = f32[1,1]{1,0:T(1,128)} slice(f32[8,128]{1,0:T(8,128)} %get-tuple-element.5), slice={[0:1], [0:1]} | slice | bytes 8 | tf_op jit(solution)/shard_map/slice | solution.py:355
  51.0 1.9 %copy.14 = bf16[8,32,1024]{2,1,0:T(8,128)(2,1)} copy(bf16[8,32,1024]{2,1,0:T(8,128)(2,1)} %bitcast.8) | data formatting | bytes 1048576

commit v4 on v3

--- a/solution.py
+++ b/solution.py
@@ -11,7 +11,7 @@
 HEADS = 16
 SMOOTHING = 0.04
 FAIRNESS = 0.95
-PIECES = 2
+PIECES = 4
 BF = jnp.bfloat16
 F32 = jnp.float32
 

time: 53.7 us -> 56.5 us (1.052); the launches traced: 52.8 us -> 56.3 us
  Pallas kernels: 47.4 us -> 50.9 us
    pallas_call x1, Pallas kernels: 47.4 us -> 50.9 us  [decode(): pl.pallas_call(functools.partial(decoder_kernel, shards, members, fields,...]
where the time goes in v4:
time: 56.5 us; the launch traced here: 56.3 us
  Pallas kernels  50.9 us (90%)
  local copies, waits for them, and re-layouts  4.8 us (8%)
  between operations  0.65 us (1%)
    pallas_call x1, Pallas kernels, decode(): pl.pallas_call(functools.partial(decoder_kernel, shards, members, fields,...  50.9 us
    unnamed x1, local copies, waits for them, and re-layouts  1.87 us
    broadcast_in_dim x4, local copies, waits for them, and re-layouts, local(): jnp.broadcast_to(request.reshape(shards, 1, cap, 1, 1), (shards, PIECES,...  1.75 us
    slice x1, local copies, waits for them, and re-layouts, local(): mean_loss = loss[0, 0:1]  1.19 us

profile of v4, /device:TPU:0, one launch (start us, length us, event | category | flops | bytes accessed | tf_op | source)
XLA Modules:
  0.0 56.3 jit_solution(3191739176688098045)
XLA Ops:
  0.6 0.8 %copy.12 = s32[16,2]{1,0:T(8,128)S(1)} copy(s32[16,2]{0,1:T(2,128)} %bitcast.9) | data formatting | bytes 256 | tf_op jit(solution)/shard_map/broadcast_in_dim | solution.py:346
  1.4 0.1 broadcast_in_dim.12
  1.5 0.1 broadcast_in_dim.13
  1.6 0.8 %broadcast_in_dim.14.ask_ref = s32[256,128]{1,0:T(8,128)} broadcast(s32[256]{0:T(256)S(1)} %broadcast_in_dim.13), dimensions={0} | broadcast | bytes 132096 | tf_op jit(solution)/shard_map/broadcast_in_dim | solution.py:346
  2.4 50.9 %shard_map.104 = (bf16[256,1024]{1,0:T(8,128)(2,1)}, f32[8,128]{1,0:T(8,128)}) custom-call(s32[256,128]{1,0:T(8,128)} %broadcast_in_dim.14.ask_ref, bf16[256,1024]{1,0:T(8,128)(2,1)} %bitcast.7, bf16[100,1024]{1,0:T(8,128)(2,1)} %fw_ref.1, f32[100,128]{1,0:T(8,128)} %target_ref.1, f32[1,128]{1,0:T(1,128)} %bitcast.10, s32[3,128]{1,0:T(4,128)} %edge_ref.1, ...), custom_call_target="tpu_custom_call" | custom-call | tf_op jit(solution)/shard_map/pallas_call | solution.py:302
  53.2 1.2 %slice.3 = f32[1,1]{1,0:T(1,128)} slice(f32[8,128]{1,0:T(8,128)} %get-tuple-element.5), slice={[0:1], [0:1]} | slice | bytes 8 | tf_op jit(solution)/shard_map/slice | solution.py:355
  54.4 1.9 %copy.14 = bf16[8,32,1024]{2,1,0:T(8,128)(2,1)} copy(bf16[8,32,1024]{2,1,0:T(8,128)(2,1)} %bitcast.8) | data formatting | bytes 1048576

commit v5 on v3

--- a/solution.py
+++ b/solution.py
@@ -171,17 +171,9 @@
             p_s[e, k] = weight
             att_s[cs, gs] = dot(values, weight.astype(BF), (0, 0)).astype(BF)
 
-    def by_pairs(work, h):
-        first = h * piece_members
-        for e in range(0, piece_members % 2):
-            work(first + e)
-
-        def step(i, carry):
-            work(first + piece_members % 2 + 2 * i)
-            work(first + piece_members % 2 + 2 * i + 1)
-            return carry
-
-        lax.fori_loop(0, piece_members // 2, step, 0)
+    def by_member(work, h):
+        for e in range(piece_members):
+            work(h * piece_members + e)
 
     kv_rows = piece_members * slots
     for h in range(PIECES):
@@ -194,7 +186,7 @@
             kv_s[h * kv_rows:(h + 1) * kv_rows, c:c + 512] = dot(
                 latent, kvw_s[:, c:c + 512], (1, 0)
             ).astype(BF)
-        by_pairs(attend, h)
+        by_member(attend, h)
     pred_s[0:fields, :] = dot(fw_ref[...], att_s[...], (1, 0))
     if padded > fields:
         pred_s[fields:padded, :] = jnp.zeros((padded - fields, members * points), F32)
@@ -263,7 +255,7 @@
 
     finish_back = []
     for h in range(PIECES):
-        by_pairs(backward, h)
+        by_member(backward, h)
         ws = slice(h * wire_rows, (h + 1) * wire_rows)
         latent_grad = dot(sg_s[h * kv_rows:(h + 1) * kv_rows, :], kvw_s[...], (1, 1)).astype(BF)
         sent = jnp.zeros((wire_rows, wide), F32)
@@ -303,7 +295,7 @@
         functools.partial(decoder_kernel, shards, members, fields, slots, cap, nodes, count),
         out_shape=(
             jax.ShapeDtypeStruct(mesh_rows.shape, BF),
-            jax.ShapeDtypeStruct((8, 128), F32),
+            jax.ShapeDtypeStruct((1, 1), F32),
         ),
         in_specs=[vmem] * 6 + [hbm] * 3,
         out_specs=(vmem, vmem),
@@ -352,7 +344,7 @@
         shards, members, cap,
     )
     mesh_grad = mesh_grad.reshape(members, nodes, width)
-    mean_loss = loss[0, 0:1]
+    mean_loss = loss.reshape(1)
     return (mesh_grad, mean_loss)
 
 

time: 53.7 us -> 52.4 us (0.976)
  between operations: 0.65 us -> 2.35 us
  Pallas kernels: 47.4 us -> 46.1 us
  local copies, waits for them, and re-layouts: 4.76 us -> 3.58 us
    pallas_call x1, Pallas kernels: 47.4 us -> 46.1 us  [decode(): pl.pallas_call(functools.partial(decoder_kernel, shards, members, fields,...]
    slice x1 -> x0, local copies, waits for them, and re-layouts: 1.19 us -> none  [local(): mean_loss = loss[0, 0:1]]
where the time goes in v5:
time: 52.4 us; the launch traced here: 52.1 us
  Pallas kernels  46.1 us (88%)
  local copies, waits for them, and re-layouts  3.58 us (7%)
  between operations  2.35 us (4%)
    pallas_call x1, Pallas kernels, decode(): pl.pallas_call(functools.partial(decoder_kernel, shards, members, fields,...  46.1 us
    unnamed x1, local copies, waits for them, and re-layouts  1.87 us
    broadcast_in_dim x4, local copies, waits for them, and re-layouts, local(): jnp.broadcast_to(request.reshape(shards, 1, cap, 1, 1), (shards, PIECES,...  1.71 us

profile of v5, /device:TPU:0, one launch (start us, length us, event | category | flops | bytes accessed | tf_op | source)
XLA Modules:
  0.0 52.1 jit_solution(1670962130880799166)
XLA Ops:
  0.6 0.8 %copy.12 = s32[16,2]{1,0:T(8,128)S(1)} copy(s32[16,2]{0,1:T(2,128)} %bitcast.9) | data formatting | bytes 256 | tf_op jit(solution)/shard_map/broadcast_in_dim | solution.py:338
  1.4 0.1 broadcast_in_dim.12
  1.5 0.1 broadcast_in_dim.13
  1.6 0.8 %broadcast_in_dim.14.ask_ref = s32[256,128]{1,0:T(8,128)} broadcast(s32[256]{0:T(256)S(1)} %broadcast_in_dim.13), dimensions={0} | broadcast | bytes 132096 | tf_op jit(solution)/shard_map/broadcast_in_dim | solution.py:338
  2.4 46.1 %shard_map.104 = (bf16[256,1024]{1,0:T(8,128)(2,1)}, f32[1,1]{1,0:T(1,128)}) custom-call(s32[256,128]{1,0:T(8,128)} %broadcast_in_dim.14.ask_ref, bf16[256,1024]{1,0:T(8,128)(2,1)} %bitcast.7, bf16[100,1024]{1,0:T(8,128)(2,1)} %fw_ref.1, f32[100,128]{1,0:T(8,128)} %target_ref.1, f32[1,128]{1,0:T(1,128)} %bitcast.10, s32[3,128]{1,0:T(4,128)} %edge_ref.1, ...), custom_call_target="tpu_custom_call" | custom-call | tf_op jit(solution)/shard_map/pallas_call | solution.py:294
  48.5 1.9 %copy.15 = bf16[8,32,1024]{2,1,0:T(8,128)(2,1)} copy(bf16[8,32,1024]{2,1,0:T(8,128)(2,1)} %bitcast.8) | data formatting | bytes 1048576
